TPU v7x, 512 devices: a whole 4x4x16 slice. The times are simulated.
512 devices in a mesh: sec: 4 (over z_hi, core), gx: 32 (over y, z_lo), gy: 4 (over x).
Axes of the slice: x: 4, y: 4, z: 16 (z_hi: 2, z_lo: 8; z = z_hi * 8 + z_lo), core: 2. Of those that a mesh axis runs over, the one named last changes fastest.
Arguments:
- adjoint: float32 [4, 5, 256, 32, 128], P('sec', None, 'gx', 'gy'), may hold values from -6 to 6
- flow: float32 [4, 6, 256, 32, 128], P('sec', None, 'gx', 'gy'), as said below
- point_cell: int32 [4, 32, 4, 1024], P('sec', 'gx', 'gy'), may hold values from 0 to 8191
- point_dest: int32 [4, 32, 4, 1024], P('sec', 'gx', 'gy'), may hold values from 0 to 127, as said below
- point_target: int32 [4, 32, 4, 1024], P('sec', 'gx', 'gy'), may hold values from 0 to 8191
- point_weight: float32 [4, 32, 4, 1024], P('sec', 'gx', 'gy'), may hold values from 0.5 to 2
- point_count: int32 [4, 32, 4], P('sec', 'gx', 'gy'), may hold values from 0 to 1024, as said below
Outputs:
- adjoint_next: float32 [4, 5, 256, 32, 128], P('sec', None, 'gx', 'gy')
Inputs may be any that keep to these rules, and one draw needn't show every extreme that they name: `flow`: density 0.6 to 1.6, pressure 0.4 (E - kinetic) from 0.5 to 1.5, sponge rate 0.05 to 1. `point_count`: zero on the near-field section; on far-field tiles a multiple of 128, reaching 1024 on some tile. `point_dest`: among the live slots of one far-field tile at most 20 name the same near-field tile, and 20 is reached. Near-field tiles receive unequal numbers of points.
All inputs are finite; a program needn't handle non-finite values.
Results may differ from a plain program's by a relative error of at most 0.00002.
Values sent between devices are 32-bit elements; how exact they have to be, the bound alone decides.
A program may use at most 64 MiB of HBM per device.

v0:
```python
import jax
import jax.numpy as jnp
from jax import lax
from jax.sharding import PartitionSpec as P

GAMMA_MINUS = 0.4
GAMMA_RATIO = 1.4
STEP_SIZE = 0.4


def extended(x, sides, width):
    for axis, dim in sides:
        count, length = (lax.axis_size(axis), x.shape[dim])
        up = [(i, (i + 1) % count) for i in range(count - 1)]
        down = [(j, i) for i, j in up]
        last = lax.slice_in_dim(x, length - width, length, axis=dim)
        initial = lax.slice_in_dim(x, 0, width, axis=dim)
        before = lax.ppermute(last, axis, up)
        after = lax.ppermute(initial, axis, down)
        x = jnp.concatenate([before, x, after], axis=dim)
    return x


def shifted(padded, offset, along):
    length = padded.shape[along] - 6
    return lax.slice_in_dim(padded, 3 + offset, 3 + offset + length, axis=along)


def stencil(padded, along):
    first = shifted(padded, 1, along) - shifted(padded, -1, along)
    second = shifted(padded, 2, along) - shifted(padded, -2, along)
    third = shifted(padded, 3, along) - shifted(padded, -3, along)
    return (45.0 * first - 9.0 * second + third) / 60.0


def wrap_last(values_in):
    return jnp.concatenate([values_in[..., -3:], values_in, values_in[..., :3]], axis=-1)


def fluxes(adjoint, flow, direction):
    density = flow[0]
    inverse = 1.0 / density
    momenta = flow[1:4]
    velocity = momenta[direction] * inverse
    kinetic = (
        0.5
        * (momenta[0] * momenta[0] + momenta[1] * momenta[1] + momenta[2] * momenta[2])
        * inverse
    )
    pressure = GAMMA_MINUS * (flow[4] - kinetic)
    stiffness = GAMMA_RATIO * pressure
    return jnp.stack(
        [
            velocity * adjoint[0],
            velocity * adjoint[1],
            velocity * adjoint[2],
            velocity * adjoint[3],
            velocity * adjoint[4],
            density * adjoint[0] + stiffness * adjoint[4],
            adjoint[1 + direction] * inverse,
        ]
    )


def masked_fluxes(adjoint, flow, direction, inside):
    safe_flow = jnp.concatenate([jnp.where(inside, flow[:1], 1.0), flow[1:]], axis=0)
    return jnp.where(inside, fluxes(adjoint, safe_flow, direction), 0.0)


def assemble(adjoint, flow, along_x, along_y, along_z, source):
    summed = along_x + along_y + along_z
    rate_list = jnp.stack(
        [
            summed[0],
            summed[1] + along_x[5],
            summed[2] + along_y[5],
            summed[3] + along_z[5],
            summed[4] + summed[6],
        ]
    )
    return adjoint + STEP_SIZE * (rate_list - flow[5] * adjoint + source)


def local(adjoint, flow, point_cell, point_dest, point_target, point_weight, point_count):
    adjoint_block = adjoint[0]
    fields = flow[0]
    channels, rows_x, rows_y, depth_cells = adjoint_block.shape
    tile_count = lax.axis_size("gx") * lax.axis_size("gy")
    slot_count = point_cell.shape[-1]
    capacity = 5 * slot_count // (2 * tile_count)
    buffer_width = tile_count * capacity
    cell_index = point_cell.reshape(slot_count)
    dest_tile = point_dest.reshape(slot_count)
    target_cell = point_target.reshape(slot_count)
    flat_block = adjoint_block.reshape(channels, -1)
    values = flat_block[:, cell_index] * point_weight.reshape(slot_count)[None, :]
    live_slot = jnp.arange(slot_count, dtype=jnp.int32) < point_count.reshape(())
    onehot = (
        (dest_tile[:, None] == jnp.arange(tile_count, dtype=jnp.int32)[None, :])
        & live_slot[:, None]
    ).astype(jnp.int32)
    slot_rank = jnp.sum(jnp.cumsum(onehot, axis=0) * onehot, axis=1) - 1
    position = jnp.where(live_slot, dest_tile * capacity + slot_rank, buffer_width)
    packed_values = (
        jnp.zeros((channels, buffer_width), jnp.float32).at[:, position].set(values, mode="drop")
    )
    packed_targets = (
        jnp.zeros((1, buffer_width), jnp.int32).at[0, position].set(target_cell, mode="drop")
    )
    tile_values, tile_targets = (
        lax.all_to_all(packed_values, ("gx", "gy"), split_axis=1, concat_axis=1, tiled=True),
        lax.all_to_all(packed_targets, ("gx", "gy"), split_axis=1, concat_axis=1, tiled=True),
    )
    merged_values, merged_targets = (
        lax.all_gather(tile_values, "sec", axis=1, tiled=True),
        lax.all_gather(tile_targets, "sec", axis=1, tiled=True),
    )
    source = jnp.zeros((channels, rows_x * rows_y * depth_cells), jnp.float32)
    source = (
        source.at[:, merged_targets[0]]
        .add(merged_values)
        .reshape(channels, rows_x, rows_y, depth_cells)
    )
    is_near = lax.axis_index("sec") == lax.axis_size("sec") - 1
    source = jnp.where(is_near, source, 0.0)
    joined = jnp.concatenate([adjoint_block, fields], axis=0)
    padded = extended(joined, (("gx", 1), ("gy", 2)), 3)
    x_position = lax.axis_index("gx") * rows_x - 3 + jnp.arange(rows_x + 6, dtype=jnp.int32)
    x_inside = (x_position >= 0) & (x_position < lax.axis_size("gx") * rows_x)
    y_position = lax.axis_index("gy") * rows_y - 3 + jnp.arange(rows_y + 6, dtype=jnp.int32)
    y_inside = (y_position >= 0) & (y_position < lax.axis_size("gy") * rows_y)
    strip_x = padded[:, :, 3:-3, :]
    flux_x = masked_fluxes(strip_x[:channels], strip_x[channels:], 0, x_inside[:, None, None])
    along_x = stencil(flux_x, 1)
    strip_y = padded[:, 3:-3, :, :]
    flux_y = masked_fluxes(strip_y[:channels], strip_y[channels:], 1, y_inside[None, :, None])
    along_y = stencil(flux_y, 2)
    along_z = stencil(wrap_last(fluxes(adjoint_block, fields, 2)), 3)
    result = assemble(adjoint_block, fields, along_x, along_y, along_z, source)
    return result[None]


def solution(mesh):
    placed = (
        P("sec", None, "gx", "gy", None),
        P("sec", None, "gx", "gy", None),
        P("sec", "gx", "gy", None),
        P("sec", "gx", "gy", None),
        P("sec", "gx", "gy", None),
        P("sec", "gx", "gy", None),
        P("sec", "gx", "gy"),
    )
    return jax.shard_map(
        local,
        mesh=mesh,
        in_specs=placed,
        out_specs=P("sec", None, "gx", "gy", None),
        check_vma=False,
    )
```

profile of v0, /device:TPU:91, one launch (start us, length us, event | category | flops | bytes accessed | tf_op | source)
XLA Modules:
  0.0 204.8 jit_solution(14550307588079525748)
XLA Ops:
  0.0 0.8 copy.17
  1.5 0.3 fusion.6
  2.1 1.2 fusion.4
  3.3 0.7 compare_select_fusion.2
  4.0 0.8 and_reduce_fusion
  4.8 0.7 fusion.72
  5.6 4.5 %scatter_custom_fusion.2 = s32[2560]{0:T(1024)S(1)} fusion(s32[1024]{0:T(1024)S(1)} %broadcast_select_fusion.3, s32[1024]{0:T(1024)} %bitcast.146, s32[]{:T(128)} %constant.27.clone.1), kind=kCustom, calls=%fused_computation.167 | custom fusion | bytes 10752
  10.0 0.7 all_to_all.16
  10.8 18.3 %all-to-all-start = ((s32[1,128,20]{2,0,1:T(1,128)}), s32[1,128,20]{2,0,1:T(1,128)S(1)}, u32[]{:S(2)}, u32[]{:S(2)}) async-start(s32[1,128,20]{2,0,1:T(1,128)} %bitcast.26), calls=%async_computation | async-start | bytes 131072 | tf_op jit(solution)/shard_map/all_to_all | solution.py:112
  29.1 1.6 pad_maximum_fusion.4
  30.7 2.2 %collective-permute-start.1 = (f32[11,3,8,128]{3,2,1,0:T(8,128)}, f32[11,3,8,128]{3,2,1,0:T(8,128)S(1)}, u32[]{:S(2)}, u32[]{:S(2)}) collective-permute-start(f32[11,3,8,128]{3,2,1,0:T(8,128)} %get-tuple-element.18), channel_id=1, source_target_pairs={{4,0},{8,4},{12,8},{16,12},{20,16},{24,20},{28,24},{32,28},{36,32}... | collective-permute-start | bytes 405512 | tf_op jit(solution)/shard_map/ppermute | solution.py:19
  32.8 3.1 %collective-permute-start = (f32[11,3,8,128]{3,2,1,0:T(8,128)S(1)}, f32[11,3,8,128]{3,2,1,0:T(8,128)S(1)}, u32[]{:S(2)}, u32[]{:S(2)}) collective-permute-start(f32[11,3,8,128]{3,2,1,0:T(8,128)S(1)} %get-tuple-element.17), channel_id=1, source_target_pairs={{0,4},{4,8},{8,12},{12,16},{16,20},{20,24},{24,28},{28,32},{32,36}... | collective-permute-start | bytes 405512 | tf_op jit(solution)/shard_map/ppermute | solution.py:18
  36.3 2.7 %copy.20 = f32[1,5,8,8,128]{1,4,3,2,0:T(8,128)} copy(f32[1,5,8,8,128]{4,3,2,1,0:T(8,128)S(1)} %copy-done) | data formatting | bytes 327680 | tf_op args[0]
  39.0 9.7 %scatter_custom_fusion = f32[5,2560]{0,1:T(8,128)S(1)} fusion(s32[1024]{0:T(1024)S(1)} %bitcast.142, f32[]{:T(128)} %constant.32.clone.1, f32[1024]{0:T(1024)S(1)} %bitcast.145, f32[5,8192]{0,1:T(8,128)} %bitcast.136, s32[1024]{0:T(1024)S(1)} %broadcast_clamp_fusion), kind=kCustom, calls=%fused_computation.7 | custom fusion | flops 5120 | bytes 223236 | tf_op jit(solution)/shard_map/scatter | solution.py:105
  48.7 0.4 copy.21
  49.1 0.4 all_to_all.19
  49.5 1.0 copy.22
  50.5 23.5 %all-to-all-start.1 = ((f32[5,128,20]{2,0,1:T(8,128)}), f32[5,128,20]{2,0,1:T(8,128)S(1)}, u32[]{:S(2)}, u32[]{:S(2)}) async-start(f32[5,128,20]{2,0,1:T(8,128)} %copy.22), calls=%async_computation.1 | async-start | bytes 1048576 | tf_op jit(solution)/shard_map/all_to_all | solution.py:111
  74.0 0.6 broadcast.293
  74.6 0.8 reduce.7
  75.6 27.9 %all_gather.6 = s32[1,10240]{1,0:T(1,128)S(1)} all-gather(s32[1,2560]{1,0:T(1,128)S(1)} %all_to_all.18), channel_id=1, replica_groups=mesh['sec'=4,'gx'=32,'gy'=4] {'sec'}, dimensions={1}, use_global_device_ids=true | all-gather | bytes 51200 | tf_op jit(solution)/shard_map/all_gather | solution.py:116
  103.6 0.9 fusion.80
  104.5 2.2 %collective-permute-start.3 = (f32[11,14,3,128]{3,2,1,0:T(4,128)}, f32[11,14,3,128]{3,2,1,0:T(4,128)S(1)}, u32[]{:S(2)}, u32[]{:S(2)}) collective-permute-start(f32[11,14,3,128]{3,2,1,0:T(4,128)} %get-tuple-element.16), channel_id=1, source_target_pairs={{1,0},{2,1},{3,2},{5,4},{6,5},{7,6},{9,8},{10,9},{11,10},{13,12},{... | collective-permute-start | bytes 709640 | tf_op jit(solution)/shard_map/ppermute | solution.py:19
  106.7 3.3 %collective-permute-start.2 = (f32[11,14,3,128]{3,2,1,0:T(4,128)}, f32[11,14,3,128]{3,2,1,0:T(4,128)S(1)}, u32[]{:S(2)}, u32[]{:S(2)}) collective-permute-start(f32[11,14,3,128]{3,2,1,0:T(4,128)} %get-tuple-element.15), channel_id=1, source_target_pairs={{0,1},{1,2},{2,3},{4,5},{5,6},{6,7},{8,9},{9,10},{10,11},{12,13},{... | collective-permute-start | bytes 709640 | tf_op jit(solution)/shard_map/ppermute | solution.py:18
  110.5 0.2 all_to_all.21
  110.8 17.0 %all_gather.7 = f32[5,10240]{1,0:T(8,128)S(1)} all-gather(f32[5,2560]{1,0:T(8,128)S(1)} %all_to_all.21), channel_id=1, replica_groups=mesh['sec'=4,'gx'=32,'gy'=4] {'sec'}, dimensions={1}, use_global_device_ids=true | all-gather | bytes 256000 | tf_op jit(solution)/shard_map/all_gather | solution.py:115
  127.7 3.1 %copy.24 = f32[10240,5]{1,0:T(8,128)} copy(f32[10240,5]{0,1:T(8,128)S(1)} %bitcast.138) | data formatting | bytes 409600 | tf_op jit(solution)/shard_map/all_gather | solution.py:115
  130.9 66.5 %scatter_custom_fusion.1 = f32[5,8192]{0,1:T(8,128)} fusion(s32[10240]{0:T(1024)S(1)} %bitcast.139, f32[10240,5]{1,0:T(8,128)} %copy.24, f32[]{:T(128)} %constant.32.clone.1), kind=kCustom, calls=%fused_computation.5 | custom fusion | flops 51200 | bytes 164352 | tf_op jit(solution)/shard_map/scatter-add | solution.py:121
  197.3 2.3 %broadcast_select_fusion = f32[5,8192]{0,1:T(8,128)} fusion(f32[5,8192]{0,1:T(8,128)} %scatter_custom_fusion.1, pred[]{:T(512)S(6)} %eq.28), kind=kLoop, calls=%fused_computation.4 | loop fusion | flops 40960 | bytes 327681 | tf_op jit(solution)/shard_map/jit(_where)/select_n | solution.py:125
  199.6 2.9 %copy.25 = f32[1,5,8,8,128]{4,3,2,1,0:T(8,128)S(1)} copy(f32[1,5,8,8,128]{1,4,3,2,0:T(8,128)} %bitcast.137) | data formatting | bytes 327680 | tf_op jit(solution)/shard_map/jit(_where)/select_n | solution.py:125
  203.3 0.7 add_add_fusion
  204.1 0.7 multiply_add_fusion
  (61 shorter events, 2.0 us)
Async XLA Ops:
  0.0 36.0 %copy-start.1 = (f32[1,6,8,8,128]{4,3,2,1,0:T(8,128)S(1)}, f32[1,6,8,8,128]{4,3,2,1,0:T(8,128)}, u32[]{:S(2)}) copy-start(f32[1,6,8,8,128]{4,3,2,1,0:T(8,128)} %param.8) | copy-start | bytes 589828
  0.0 36.0 %copy-start = (f32[1,5,8,8,128]{4,3,2,1,0:T(8,128)S(1)}, f32[1,5,8,8,128]{4,3,2,1,0:T(8,128)}, u32[]{:S(2)}) copy-start(f32[1,5,8,8,128]{4,3,2,1,0:T(8,128)} %param.7) | copy-start | bytes 491524
  0.0 36.0 %copy-start.2 = (s32[1,1,1,1024]{3,2,1,0:T(1,128)S(1)}, s32[1,1,1,1024]{3,2,1,0:T(1,128)}, u32[]{:S(2)}) copy-start(s32[1,1,1,1024]{3,2,1,0:T(1,128)} %param.9) | copy-start | bytes 12292
  2.0 37.0 %copy-start.3 = (f32[1,1,1,1024]{3,2,1,0:T(1,128)S(1)}, f32[1,1,1,1024]{3,2,1,0:T(1,128)}, u32[]{:S(2)}) copy-start(f32[1,1,1,1024]{3,2,1,0:T(1,128)} %param.12) | copy-start | bytes 12292
  10.8 39.7 %all-to-all-start = ((s32[1,128,20]{2,0,1:T(1,128)}), s32[1,128,20]{2,0,1:T(1,128)S(1)}, u32[]{:S(2)}, u32[]{:S(2)}) async-start(s32[1,128,20]{2,0,1:T(1,128)} %bitcast.26), calls=%async_computation | async-start | bytes 131072 | tf_op jit(solution)/shard_map/all_to_all | solution.py:112
  30.7 72.8 %collective-permute-start.1 = (f32[11,3,8,128]{3,2,1,0:T(8,128)}, f32[11,3,8,128]{3,2,1,0:T(8,128)S(1)}, u32[]{:S(2)}, u32[]{:S(2)}) collective-permute-start(f32[11,3,8,128]{3,2,1,0:T(8,128)} %get-tuple-element.18), channel_id=1, source_target_pairs={{4,0},{8,4},{12,8},{16,12},{20,16},{24,20},{28,24},{32,28},{36,32}... | collective-permute-start | bytes 405512 | tf_op jit(solution)/shard_map/ppermute | solution.py:19
  32.8 70.7 %collective-permute-start = (f32[11,3,8,128]{3,2,1,0:T(8,128)S(1)}, f32[11,3,8,128]{3,2,1,0:T(8,128)S(1)}, u32[]{:S(2)}, u32[]{:S(2)}) collective-permute-start(f32[11,3,8,128]{3,2,1,0:T(8,128)S(1)} %get-tuple-element.17), channel_id=1, source_target_pairs={{0,4},{4,8},{8,12},{12,16},{16,20},{20,24},{24,28},{28,32},{32,36}... | collective-permute-start | bytes 405512 | tf_op jit(solution)/shard_map/ppermute | solution.py:18
  50.5 60.0 %all-to-all-start.1 = ((f32[5,128,20]{2,0,1:T(8,128)}), f32[5,128,20]{2,0,1:T(8,128)S(1)}, u32[]{:S(2)}, u32[]{:S(2)}) async-start(f32[5,128,20]{2,0,1:T(8,128)} %copy.22), calls=%async_computation.1 | async-start | bytes 1048576 | tf_op jit(solution)/shard_map/all_to_all | solution.py:111
  104.5 98.0 %collective-permute-start.3 = (f32[11,14,3,128]{3,2,1,0:T(4,128)}, f32[11,14,3,128]{3,2,1,0:T(4,128)S(1)}, u32[]{:S(2)}, u32[]{:S(2)}) collective-permute-start(f32[11,14,3,128]{3,2,1,0:T(4,128)} %get-tuple-element.16), channel_id=1, source_target_pairs={{1,0},{2,1},{3,2},{5,4},{6,5},{7,6},{9,8},{10,9},{11,10},{13,12},{... | collective-permute-start | bytes 709640 | tf_op jit(solution)/shard_map/ppermute | solution.py:19
  106.7 95.8 %collective-permute-start.2 = (f32[11,14,3,128]{3,2,1,0:T(4,128)}, f32[11,14,3,128]{3,2,1,0:T(4,128)S(1)}, u32[]{:S(2)}, u32[]{:S(2)}) collective-permute-start(f32[11,14,3,128]{3,2,1,0:T(4,128)} %get-tuple-element.15), channel_id=1, source_target_pairs={{0,1},{1,2},{2,3},{4,5},{5,6},{6,7},{8,9},{9,10},{10,11},{12,13},{... | collective-permute-start | bytes 709640 | tf_op jit(solution)/shard_map/ppermute | solution.py:18
where the time goes:
time: 205 us
  other arithmetic  87.6 us (43%)
  starting transfers between devices  52.5 us (26%)
  blocking collectives  44.9 us (22%)
  local copies, waits for them, and re-layouts  18.7 us (9%)
    scatter-add x1, other arithmetic, local(): source = source.at[:, merged_targets[0]].add(merged_values).reshape(chann...  66.5 us
    all_gather x1, blocking collectives, local(): lax.all_gather(tile_targets, 'sec', axis=1, tiled=True)  27.9 us
    all_to_all x1, starting transfers between devices, local(): lax.all_to_all(packed_values, ('gx', 'gy'), split_axis=1, concat_axis=1,...  23.5 us
    all_to_all x1, starting transfers between devices, local(): lax.all_to_all(packed_targets, ('gx', 'gy'), split_axis=1, concat_axis=1,...  18.3 us
    all_gather x1, blocking collectives, local(): lax.all_gather(tile_values, 'sec', axis=1, tiled=True)  17 us
    scatter x1, other arithmetic, local(): jnp.zeros((channels, buffer_width), jnp.float32).at[:, position]  9.7 us
    unnamed x11, local copies, waits for them, and re-layouts  7.16 us
    ppermute x2, starting transfers between devices, extended(): before = lax.ppermute(last, axis, up)  6.37 us
  transfers between devices with their start and end apart: 6, of which 0 were waited for; matrix products, arithmetic and copies ran while one was open for 46% of the time, Pallas kernels for 0%

commit v1 on v0

--- a/solution.py
+++ b/solution.py
@@ -6,6 +6,12 @@
 GAMMA_MINUS = 0.4
 GAMMA_RATIO = 1.4
 STEP_SIZE = 0.4
+
+
+def balance_skins(s0, axis_tag):
+    field_out = lax.axis_size(axis_tag)
+    block_last = jnp.split(s0, field_out, 1)
+    return jnp.concatenate(lax.all_to_all(jnp.stack(block_last, 0), axis_tag, 0, 0), 1)
 
 
 def extended(x, sides, width):
@@ -108,7 +114,7 @@
         jnp.zeros((1, buffer_width), jnp.int32).at[0, position].set(target_cell, mode="drop")
     )
     tile_values, tile_targets = (
-        lax.all_to_all(packed_values, ("gx", "gy"), split_axis=1, concat_axis=1, tiled=True),
+        balance_skins(packed_values, ("gx", "gy")),
         lax.all_to_all(packed_targets, ("gx", "gy"), split_axis=1, concat_axis=1, tiled=True),
     )
     merged_values, merged_targets = (

time: 205 us -> 314 us (1.53)
  local copies, waits for them, and re-layouts: 18.7 us -> 125 us
    unnamed x11 -> x138, local copies, waits for them, and re-layouts: 7.16 us -> 82.2 us
    split x0 -> x135, local copies, waits for them, and re-layouts: none -> 33.1 us  [balance_skins(): block_last = jnp.split(s0, field_out, 1)]
  transfers between devices with their start and end apart: 6 -> 6, of which waited for: 0 -> 0; matrix products, arithmetic and copies ran while one was open for 46% -> 64% of each run, Pallas kernels for 0% -> 0%
where the time goes in v1:
time: 314 us; the launch traced here: 312 us
  local copies, waits for them, and re-layouts  125 us (40%)
  other arithmetic  87.5 us (28%)
  starting transfers between devices  52.4 us (17%)
  blocking collectives  45 us (14%)
    unnamed x138, local copies, waits for them, and re-layouts  82.2 us
    scatter-add x1, other arithmetic, local(): source = source.at[:, merged_targets[0]].add(merged_values).reshape(chann...  66.5 us
    split x135, local copies, waits for them, and re-layouts, balance_skins(): block_last = jnp.split(s0, field_out, 1)  33.1 us
    all_gather x1, blocking collectives, local(): lax.all_gather(tile_targets, 'sec', axis=1, tiled=True)  28.1 us
    all_to_all x1, starting transfers between devices, balance_skins(): lax.all_to_all(jnp.stack(block_last, 0), axis_tag, 0, 0)  23.5 us
    all_to_all x1, starting transfers between devices, local(): lax.all_to_all(packed_targets, ('gx', 'gy'), split_axis=1, concat_axis=1,...  18.3 us
    all_gather x1, blocking collectives, local(): lax.all_gather(tile_values, 'sec', axis=1, tiled=True)  17 us
    scatter x1, other arithmetic, local(): jnp.zeros((channels, buffer_width), jnp.float32).at[:, position]  9.69 us
  transfers between devices with their start and end apart: 6, of which 0 were waited for; matrix products, arithmetic and copies ran while one was open for 64% of the time, Pallas kernels for 0%

profile of v1, /device:TPU:91, one launch (start us, length us, event | category | flops | bytes accessed | tf_op | source)
XLA Modules:
  0.0 311.6 jit_solution(4669498610223915699)
XLA Ops:
  0.0 0.8 copy.800
  2.1 1.2 fusion.4
  5.5 4.5 %scatter_custom_fusion.2 = s32[2560]{0:T(1024)S(1)} fusion(s32[1024]{0:T(1024)S(1)} %broadcast_select_fusion.3, s32[1024]{0:T(1024)} %bitcast.404, s32[]{:T(128)} %constant.27.clone.1), kind=kCustom, calls=%fused_computation.295 | custom fusion | bytes 10752
  10.8 18.3 %all-to-all-start = ((s32[1,128,20]{2,0,1:T(1,128)}), s32[1,128,20]{2,0,1:T(1,128)S(1)}, u32[]{:S(2)}, u32[]{:S(2)}) async-start(s32[1,128,20]{2,0,1:T(1,128)} %bitcast.26), calls=%async_computation | async-start | bytes 131072 | tf_op jit(solution)/shard_map/all_to_all | solution.py:118
  29.1 1.0 pad_maximum_fusion.4
  30.0 2.2 collective-permute-start.1
  32.2 3.1 %collective-permute-start = (f32[11,3,8,128]{3,2,1,0:T(8,128)S(1)}, f32[11,3,8,128]{3,2,1,0:T(8,128)S(1)}, u32[]{:S(2)}, u32[]{:S(2)}) collective-permute-start(f32[11,3,8,128]{3,2,1,0:T(8,128)S(1)} %get-tuple-element.145), channel_id=1, source_target_pairs={{0,4},{4,8},{8,12},{12,16},{16,20},{20,24},{24,28},{28,32},{32,36}... | collective-permute-start | bytes 405512 | tf_op jit(solution)/shard_map/ppermute | solution.py:24
  35.3 2.7 copy.803
  38.0 9.7 %scatter_custom_fusion = f32[5,2560]{0,1:T(8,128)S(1)} fusion(s32[1024]{0:T(1024)S(1)} %bitcast.400, f32[]{:T(128)} %constant.32.clone.1, f32[1024]{0:T(1024)S(1)} %bitcast.403, f32[5,8192]{0,1:T(8,128)} %bitcast.393, s32[1024]{0:T(1024)S(1)} %broadcast_clamp_fusion), kind=kCustom, calls=%fused_computation.7 | custom fusion | flops 5120 | bytes 223236 | tf_op jit(solution)/shard_map/scatter | solution.py:111
  51.1 0.8 copy.818
  51.9 0.8 copy.819
  52.7 0.8 copy.820
  53.5 0.8 copy.821
  54.3 0.8 copy.822
  55.1 0.8 copy.823
  55.9 0.8 copy.824
  56.7 0.8 copy.825
  57.4 0.8 copy.826
  58.2 0.8 copy.827
  59.0 0.8 copy.828
  70.9 0.8 copy.843
  156.9 23.5 %all-to-all-start.1 = ((f32[128,5,20]{2,1,0:T(8,128)}), f32[128,5,20]{2,1,0:T(8,128)S(1)}, u32[]{:S(2)}, u32[]{:S(2)}) async-start(f32[128,5,20]{2,1,0:T(8,128)} %constant_dynamic-update-slice_fusion.26), calls=%async_computation.1 | async-start | bytes 1048576 | tf_op jit(solution)/shard_map/all_to_all | solution.py:14
  180.9 0.8 reduce.7
  181.8 28.1 %all_gather.6 = s32[1,10240]{1,0:T(1,128)S(1)} all-gather(s32[1,2560]{1,0:T(1,128)S(1)} %all_to_all.13), channel_id=1, replica_groups=mesh['sec'=4,'gx'=32,'gy'=4] {'sec'}, dimensions={1}, use_global_device_ids=true | all-gather | bytes 51200 | tf_op jit(solution)/shard_map/all_gather | solution.py:122
  210.6 0.8 fusion.80
  211.5 2.2 collective-permute-start.3
  213.7 3.1 collective-permute-start.2
  217.5 17.0 %all_gather.7 = f32[5,10240]{1,0:T(8,128)S(1)} all-gather(f32[5,2560]{1,0:T(8,128)S(1)} %reshape.407), channel_id=1, replica_groups=mesh['sec'=4,'gx'=32,'gy'=4] {'sec'}, dimensions={1}, use_global_device_ids=true | all-gather | bytes 256000 | tf_op jit(solution)/shard_map/all_gather | solution.py:121
  234.5 3.1 %copy.933 = f32[10240,5]{1,0:T(8,128)} copy(f32[10240,5]{0,1:T(8,128)S(1)} %bitcast.396) | data formatting | bytes 409600 | tf_op jit(solution)/shard_map/all_gather | solution.py:121
  237.6 66.5 %scatter_custom_fusion.1 = f32[5,8192]{0,1:T(8,128)} fusion(s32[10240]{0:T(1024)} %bitcast.397, f32[10240,5]{1,0:T(8,128)} %copy.933, f32[]{:T(128)} %constant.32.clone.1), kind=kCustom, calls=%fused_computation.5 | custom fusion | flops 51200 | bytes 164352 | tf_op jit(solution)/shard_map/scatter-add | solution.py:127
  304.1 2.3 broadcast_select_fusion
  306.3 2.9 copy.934
  (321 shorter events, 107.2 us)
Async XLA Ops:
  0.0 35.3 %copy-start = (f32[1,5,8,8,128]{4,3,2,1,0:T(8,128)S(1)}, f32[1,5,8,8,128]{4,3,2,1,0:T(8,128)}, u32[]{:S(2)}) copy-start(f32[1,5,8,8,128]{4,3,2,1,0:T(8,128)} %param.7) | copy-start | bytes 491524
  1.5 36.5 %copy-start.2 = (s32[1,1,1,1024]{3,2,1,0:T(1,128)S(1)}, s32[1,1,1,1024]{3,2,1,0:T(1,128)}, u32[]{:S(2)}) copy-start(s32[1,1,1,1024]{3,2,1,0:T(1,128)} %param.9) | copy-start | bytes 12292
  1.5 36.5 %copy-start.3 = (f32[1,1,1,1024]{3,2,1,0:T(1,128)S(1)}, f32[1,1,1,1024]{3,2,1,0:T(1,128)}, u32[]{:S(2)}) copy-start(f32[1,1,1,1024]{3,2,1,0:T(1,128)} %param.12) | copy-start | bytes 12292
  10.8 146.1 %all-to-all-start = ((s32[1,128,20]{2,0,1:T(1,128)}), s32[1,128,20]{2,0,1:T(1,128)S(1)}, u32[]{:S(2)}, u32[]{:S(2)}) async-start(s32[1,128,20]{2,0,1:T(1,128)} %bitcast.26), calls=%async_computation | async-start | bytes 131072 | tf_op jit(solution)/shard_map/all_to_all | solution.py:118
  30.0 180.6 %collective-permute-start.1 = (f32[11,3,8,128]{3,2,1,0:T(8,128)S(1)}, f32[11,3,8,128]{3,2,1,0:T(8,128)S(1)}, u32[]{:S(2)}, u32[]{:S(2)}) collective-permute-start(f32[11,3,8,128]{3,2,1,0:T(8,128)S(1)} %get-tuple-element.146), channel_id=1, source_target_pairs={{4,0},{8,4},{12,8},{16,12},{20,16},{24,20},{28,24},{32,28},{36,32}... | collective-permute-start | bytes 405512 | tf_op jit(solution)/shard_map/ppermute | solution.py:25
  32.2 178.4 %collective-permute-start = (f32[11,3,8,128]{3,2,1,0:T(8,128)S(1)}, f32[11,3,8,128]{3,2,1,0:T(8,128)S(1)}, u32[]{:S(2)}, u32[]{:S(2)}) collective-permute-start(f32[11,3,8,128]{3,2,1,0:T(8,128)S(1)} %get-tuple-element.145), channel_id=1, source_target_pairs={{0,4},{4,8},{8,12},{12,16},{16,20},{20,24},{24,28},{28,32},{32,36}... | collective-permute-start | bytes 405512 | tf_op jit(solution)/shard_map/ppermute | solution.py:24
  38.0 11.2 %copy-start.1 = (f32[1,6,8,8,128]{4,3,2,1,0:T(8,128)S(1)}, f32[1,6,8,8,128]{4,3,2,1,0:T(8,128)}, u32[]{:S(2)}) copy-start(f32[1,6,8,8,128]{4,3,2,1,0:T(8,128)} %param.8) | copy-start | bytes 589828
  156.9 60.4 %all-to-all-start.1 = ((f32[128,5,20]{2,1,0:T(8,128)}), f32[128,5,20]{2,1,0:T(8,128)S(1)}, u32[]{:S(2)}, u32[]{:S(2)}) async-start(f32[128,5,20]{2,1,0:T(8,128)} %constant_dynamic-update-slice_fusion.26), calls=%async_computation.1 | async-start | bytes 1048576 | tf_op jit(solution)/shard_map/all_to_all | solution.py:14
  211.5 97.8 %collective-permute-start.3 = (f32[11,14,3,128]{3,2,1,0:T(4,128)}, f32[11,14,3,128]{3,2,1,0:T(4,128)S(1)}, u32[]{:S(2)}, u32[]{:S(2)}) collective-permute-start(f32[11,14,3,128]{3,2,1,0:T(4,128)} %get-tuple-element.144), channel_id=1, source_target_pairs={{1,0},{2,1},{3,2},{5,4},{6,5},{7,6},{9,8},{10,9},{11,10},{13,12},{... | collective-permute-start | bytes 709640 | tf_op jit(solution)/shard_map/ppermute | solution.py:25
  213.7 95.6 %collective-permute-start.2 = (f32[11,14,3,128]{3,2,1,0:T(4,128)S(1)}, f32[11,14,3,128]{3,2,1,0:T(4,128)S(1)}, u32[]{:S(2)}, u32[]{:S(2)}) collective-permute-start(f32[11,14,3,128]{3,2,1,0:T(4,128)S(1)} %get-tuple-element.143), channel_id=1, source_target_pairs={{0,1},{1,2},{2,3},{4,5},{5,6},{6,7},{8,9},{9,10},{10,11},{12,13},{... | collective-permute-start | bytes 709640 | tf_op jit(solution)/shard_map/ppermute | solution.py:24
